TPU v7x, 256 devices: a whole 4x4x8 slice. The times are simulated.
256 devices in a mesh: dp: 2 (over core), row: 16 (over y, x), col: 8 (over z).
Axes of the slice: x: 4, y: 4, z: 8, core: 2. Of those that a mesh axis runs over, the one named last changes fastest.
Arguments:
- ffn_input: bfloat16 [2, 1280, 4096], P('dp', None, 'row'), may hold values from -6 to 6
- gate_act: bfloat16 [2, 1280, 14336], P('dp', 'row', 'col'), may hold values from -8 to 8
- up_act: bfloat16 [2, 1280, 14336], P('dp', 'row', 'col'), may hold values from -6 to 6
- hidden_grad: bfloat16 [2, 1280, 14336], P('dp', 'row', 'col'), may hold values from -0.29882812 to 0.29882812
- stream_grad: bfloat16 [2, 1280, 4096], P('dp', None, 'row'), may hold values from -0.29882812 to 0.29882812
- w_gate: bfloat16 [4096, 14336], P('row', 'col'), may hold values from -0.09375 to 0.09375
- w_up: bfloat16 [4096, 14336], P('row', 'col'), may hold values from -0.09375 to 0.09375
- gate_keep: int32 [32, 112], P('row', 'col'), may hold values 0 or 1
- up_keep: int32 [32, 112], P('row', 'col'), may hold values 0 or 1
- w_out: bfloat16 [8192, 4096], P('col', 'row'), may hold values from -0.0625 to 0.0625
- queries: bfloat16 [2, 1280, 8192], P('dp', 'row', 'col'), may hold values from -6 to 6
- keys: bfloat16 [2, 1280, 1024], P('dp', 'row', 'col'), may hold values from -6 to 6
- values: bfloat16 [2, 1280, 1024], P('dp', 'row', 'col'), may hold values from -6 to 6
Outputs:
- grad_w_gate: bfloat16 [4096, 14336], P('row', 'col')
- grad_w_up: bfloat16 [4096, 14336], P('row', 'col')
- query_grad: bfloat16 [2, 1280, 8192], P('dp', 'row', 'col')
- key_grad: bfloat16 [2, 1280, 1024], P('dp', 'row', 'col')
- value_grad: bfloat16 [2, 1280, 1024], P('dp', 'row', 'col')
Inputs may be any that keep to these rules, and one draw needn't show every extreme that they name: `gate_keep`: 1 marks a trained 128 x 128 block. `up_keep`: 1 marks a trained 128 x 128 block.
All inputs are finite; a program needn't handle non-finite values.
Results may differ from a plain program's by a relative error of at most 0.039.
Values may be sent and summed in bfloat16 or wider, within the bound.
A program may use at most 128 MiB of HBM per device.

v0:
```python
import math

import jax
import jax.numpy as jnp
from jax import lax
from jax.experimental import pallas as pl
from jax.experimental.pallas import tpu as pltpu
from jax.sharding import PartitionSpec as P

MESH = pl.DeviceIdType.MESH
F32 = jnp.float32
BF16 = jnp.bfloat16

ROWS = 80
PARTS = 4
HID = 1792
HALF = 896
FEAT = 256
SEQ = 1280
HEADS = 8
HD = 128
QS = HEADS * ROWS
SCALE = 1.0 / math.sqrt(HD)
NEGATIVE_FILL = -1e30
N_GROUPS = 46
OFFSETS = (-1, 1, 2)

QUARTERS = (
    ((0, 0), (0, -1), (-1, 0), (-1, -1)),
    ((0, 1), (1, 0), (-1, 1), (1, -1)),
    ((0, 2), (2, 0), (1, 2), (2, 1)),
    ((1, 1), (-1, 2), (2, -1), (2, 2)),
)

def pick(table, j):
    total = 0
    for k, value in enumerate(table):
        total = total + value * (1 - lax.div(lax.rem(j + (4 - k), 4) + 3, 4))
    return total


def nt(left, right):
    return lax.dot_general(left, right, (((1,), (1,)), ((), ())), preferred_element_type=F32)


def nn(left, right):
    return lax.dot_general(left, right, (((1,), (0,)), ((), ())), preferred_element_type=F32)


def kernel(
    ffn_hbm,
    gate_ref,
    up_ref,
    hidden_ref,
    stream_hbm,
    wg_hbm,
    wu_hbm,
    gk_ref,
    uk_ref,
    wo_hbm,
    q_hbm,
    k_ref,
    v_ref,
    gw_hbm,
    uw_hbm,
    dq_ref,
    dk_ref,
    dv_ref,
    ga,
    ua,
    k_all,
    v_all,
    w_eff,
    ffn_v,
    ffn_t,
    wout_v,
    q_v,
    q_s,
    stream_v,
    zs,
    zr,
    strm,
    hp,
    ra,
    rb,
    ha,
    hb,
    ra2,
    rb2,
    g_own,
    g_s,
    w_send,
    w_recv,
    w_out_v,
    k_t,
    v_t,
    out_t,
    p_f,
    p_low,
    ds_s,
    kt_s,
    vt_s,
    kt_r,
    vt_r,
    kt2_s,
    vt2_s,
    kt2_r,
    vt2_r,
    send_sem,
    recv_sem,
    local_sem,
):
    row = lax.axis_index("row")
    z = lax.axis_index("col")
    core = lax.axis_index("dp")
    y, x = row // 4, row % 4

    def ring(v, off):
        return lax.rem(v + (off + 4), 4)

    def dev(axis, off):
        if axis == "x":
            return {"row": y * 4 + ring(x, off)}
        return {"row": ring(y, off) * 4 + x}

    groups = []

    class Group:
        def __init__(self, size):
            self.i, self.size = len(groups), size
            groups.append(self)

        def copy(self, src, dst, device):
            return pltpu.make_async_remote_copy(
                src_ref=src,
                dst_ref=dst,
                send_sem=send_sem.at[self.i],
                recv_sem=recv_sem.at[self.i],
                device_id=device,
                device_id_type=MESH,
            )

        def send(self, src, dst, device):
            self.copy(src, dst, device).start()

        def wait_recv(self):
            self.copy(self.size, self.size, {"dp": 1 - core}).wait_recv()

        def wait_send(self):
            self.copy(self.size, self.size, {"dp": 1 - core}).wait_send()

    barrier = pltpu.get_barrier_semaphore()
    partners = [dev("x", o) for o in OFFSETS] + [dev("y", o) for o in OFFSETS]
    partners += [{"col": lax.rem(z + o, 8)} for o in range(1, 8)] + [{"dp": 1 - core}]
    for partner in partners:
        pl.semaphore_signal(barrier, inc=1, device_id=partner, device_id_type=MESH)

    def fetch(i, src, dst):
        copy = pltpu.make_async_copy(src, dst, local_sem.at[i])
        copy.start()
        return copy

    def place(chunk):
        dy, dx = chunk
        return lax.rem(y + dy + 4, 4), lax.rem(x + dx + 4, 4)

    mine = []
    for quarter in QUARTERS:
        mine.append(place([pick([chunk[i] for chunk in quarter], z // 2) for i in range(2)]))
    side = lax.rem(z, 2)
    side_cols = pl.ds(pl.multiple_of(side * HD, HD), HD)
    get_wg = fetch(0, wg_hbm, w_eff.at[0])
    get_wu = fetch(1, wu_hbm, w_eff.at[1])
    get_ffn = fetch(2, ffn_hbm.at[0], ffn_v)
    get_wo = fetch(3, wo_hbm, wout_v)
    get_q = fetch(4, q_hbm.at[0], q_v)
    get_st = [
        fetch(5 + b, stream_hbm.at[mine[b][0] * 4 + mine[b][1], :, side_cols], stream_v.at[b])
        for b in range(4)
    ]

    def act_step(i, _):
        cols = pl.ds(pl.multiple_of(i * 128, 128), 128)
        gate_f = gate_ref[0, :, cols].astype(F32)
        hidden_f = hidden_ref[0, :, cols].astype(F32)
        sigma = jax.nn.sigmoid(gate_f)
        ua[y, x, :, cols] = (hidden_f * gate_f * sigma).astype(BF16)
        ga[y, x, :, cols] = (
            hidden_f * up_ref[0, :, cols].astype(F32) * sigma * (1.0 + gate_f * (1.0 - sigma))
        ).astype(BF16)
        return 0

    lax.fori_loop(0, HID // 128, act_step, 0, unroll=7)
    k_all[y, x] = k_ref[0]
    v_all[y, x] = v_ref[0]

    pl.semaphore_wait(barrier, len(partners))

    arrays = ((ga, "x", "y"), (ua, "y", "x"))

    def at(n, first, second):
        arr, p, _ = arrays[n]
        if p == "x":
            return arr.at[ring(y, second), ring(x, first)]
        return arr.at[ring(y, first), ring(x, second)]

    two_chunks = ga.at[0, 0:2]
    along = {(n, d): Group(at(n, 0, 0)) for n in range(2) for d in (1, -1)}
    relay = [Group(at(n, 2, 0)) for n in range(2)]
    across = {(n, first): Group(two_chunks) for n in range(2) for first in (0, -1, 1, 2)}
    far = {(n, part): Group(two_chunks) for n in range(2) for part in range(2)}

    def spread(n, first):
        block = at(n, first, 0)
        for d in (1, -1):
            across[n, first].send(block, block, dev(arrays[n][2], d))

    for n in range(2):
        for d in (1, -1):
            along[n, d].send(at(n, 0, 0), at(n, 0, 0), dev(arrays[n][1], d))
    for n in range(2):
        spread(n, 0)

    keys1, values1 = Group(k_all.at[0, 0:3]), Group(v_all.at[0, 0:3])
    keys2, values2 = Group(k_all.at[0:3]), Group(v_all.at[0:3])

    for n, (get, keep) in enumerate(((get_wg, gk_ref), (get_wu, uk_ref))):
        get.wait()

        def mask_step(j, _, n=n, keep=keep):
            cols = pl.ds(pl.multiple_of(j * 128, 128), 128)
            for i in range(2):
                rows = slice(i * 128, (i + 1) * 128)
                tile = w_eff[n, rows, cols].astype(F32) * keep[i, j].astype(F32)
                w_eff[n, rows, cols] = tile.astype(BF16)
            return 0

        lax.fori_loop(0, HID // 128, mask_step, 0)

    for d in (1, -1):
        for n in range(2):
            along[n, d].wait_recv()
            cols = slice(0, HALF) if d == 1 else slice(HALF, HID)
            part = at(n, -d, 0).at[:, cols]
            relay[n].send(part, part, dev(arrays[n][1], d))
            spread(n, -d)

    get_ffn.wait()

    def transpose_step(i, _):
        rows = pl.ds(pl.multiple_of(i * 256, 256), 256)
        ffn_t[:, rows] = ffn_v[rows, :].T
        return 0

    lax.fori_loop(0, SEQ // 256, transpose_step, 0)
    get_q.wait()
    for h in range(HEADS):
        q_s[h * ROWS : (h + 1) * ROWS, :] = q_v[:, h * HD : (h + 1) * HD]

    for n in range(2):
        relay[n].wait_recv()
        spread(n, 2)

    col_sum = [Group(zr.at[b]) for b in range(4)]
    col_all = [Group(zr.at[b]) for b in range(4)]

    def terms(n, chunks):
        spots = [place(c) for c in chunks]
        rows = jnp.concatenate([arrays[n][0][yc, xc, :, :] for yc, xc in spots], axis=0)
        return nt(rows, w_eff[n])

    def send_sums(b, i, total):
        for j in range(2):
            zs[b, i * 2 + j] = total[:, j * HD : (j + 1) * HD].astype(BF16)

    def scatter_col(b):
        for off in range(1, 8):
            to = lax.rem(z + off, 8)
            col_sum[b].send(zs.at[b, to], zr.at[b, off - 1], {"col": to})

    def input_terms(b):
        total = terms(0, QUARTERS[b]) + terms(1, QUARTERS[b])
        for i in range(4):
            send_sums(b, i, total[i * ROWS : (i + 1) * ROWS])
        scatter_col(b)

    def gather_col(b):
        col_sum[b].wait_recv()
        get_st[b].wait()
        total = zs[b, z].astype(F32)
        for j in range(7):
            total += zr[b, j].astype(F32)
        yc, xc = mine[b]
        strm[yc, xc, side] = (stream_v[b].astype(F32) + total).astype(BF16)
        block = strm.at[yc, xc, side]
        for off in range(1, 8):
            col_all[b].send(block, block, {"col": lax.rem(z + off, 8)})

    first_a = {dy: Group(ra2) for dy in (0, -1, 1, 2)}
    first_b = {dx: Group(rb2) for dx in (0, -1, 1, 2)}

    def head_terms(b, at_once=True):
        col_all[b].wait_recv()
        spots = [place(c) for c in QUARTERS[b]]
        total = jnp.concatenate(
            [
                jnp.concatenate([strm[yc, xc, j] for yc, xc in spots], axis=0) for j in range(2)
            ],
            axis=1,
        )

        def step(t, _):
            cols = pl.ds(pl.multiple_of(t * 256, 256), 256)
            part = nt(total, wout_v[cols, :]).astype(BF16)
            for i, (yc, xc) in enumerate(spots):
                hp[yc, xc, :, cols] = part[i * ROWS : (i + 1) * ROWS, :]
            return 0

        lax.fori_loop(0, 2, step, 0)
        if at_once:
            send_a(b)
        lax.fori_loop(2, 4, step, 0)
        if at_once:
            send_b(b)

    def send_a(b):
        for dy, dx in QUARTERS[b][::-1]:
            yc, xc = place((dy, dx))
            if dx != 0:
                first_a[dy].send(
                    hp.at[yc, xc, :, 0:512], ra.at[OFFSETS.index(dx), yc], dev("x", dx)
                )

    def send_b(b):
        for dy, dx in QUARTERS[b][::-1]:
            yc, xc = place((dy, dx))
            if dy != 0:
                first_b[dx].send(
                    hp.at[yc, xc, :, 512:1024], rb.at[OFFSETS.index(dy), xc], dev("y", dy)
                )

    for first, d, part in ((0, 1, 0), (-1, 1, 1), (1, -1, 0), (2, -1, 1)):
        for n in range(2):
            across[n, first].wait_recv()
            block = at(n, first, -d)
            far[n, part].send(block, block, dev(arrays[n][2], d))
        if first == -1:
            input_terms(0)
        if first == 1:
            input_terms(1)

    for o in OFFSETS:
        keys1.send(k_all.at[y, x], k_all.at[y, x], dev("x", o))
        values1.send(v_all.at[y, x], v_all.at[y, x], dev("y", o))

    gather_col(0)
    gather_col(1)
    get_wo.wait()
    head_terms(0, at_once=False)
    for n in range(2):
        far[n, 0].wait_recv()
    input_terms(2)
    for n in range(2):
        far[n, 1].wait_recv()
    input_terms(3)
    keys1.wait_recv()
    values1.wait_recv()
    for o in OFFSETS:
        keys2.send(k_all.at[y], k_all.at[y], dev("y", o))
        values2.send(v_all.at[:, x], v_all.at[:, x], dev("x", o))
    send_a(0)
    send_b(0)

    def wgrad(n):
        arr = arrays[n][0]

        def step(t, _):
            cols = pl.ds(pl.multiple_of(t * 256, 256), 256)
            tokens = arr[:, :, :, cols].reshape(SEQ, 256)
            w_send[n, :, cols] = nn(ffn_t[...], tokens).astype(BF16)
            return 0

        lax.fori_loop(0, HID // 256, step, 0)
        pair[n].send(w_send.at[n], w_recv.at[n], {"dp": 1 - core})

    pair = [Group(w_recv.at[n]) for n in range(2)]
    head_terms(1)
    gather_col(2)
    wgrad(0)
    gather_col(3)
    head_terms(2)
    head_terms(3)
    wgrad(1)

    keys2.wait_recv()
    values2.wait_recv()
    k_t[...] = k_all[...].reshape(SEQ, HD).T
    v_t[...] = v_all[...].reshape(SEQ, HD).T

    def softmax_step(t, _):
        cols = pl.ds(pl.multiple_of(t * 128, 128), 128)
        scores = nt(k_all[...].reshape(SEQ, HD), q_s[cols, :]) * SCALE
        lane = lax.broadcasted_iota(jnp.int32, (1, 128), 1) + t * 128
        head = jnp.zeros_like(lane)
        for h in range(1, HEADS):
            head += (lane >= h * ROWS).astype(jnp.int32)
        query_pos = lane - head * ROWS + row * ROWS
        key_pos = lax.broadcasted_iota(jnp.int32, (SEQ, 128), 0)
        scores = jnp.where(key_pos <= query_pos, scores, NEGATIVE_FILL)
        weight = jnp.exp(scores - jnp.max(scores, axis=0, keepdims=True))
        probs = weight * (1.0 / jnp.sum(weight, axis=0, keepdims=True))
        p_f[:, cols] = probs
        p_low[:, cols] = probs.astype(BF16)
        out_t[:, cols] = nn(v_t[...], p_low[:, cols])
        return 0

    lax.fori_loop(0, QS // 128, softmax_step, 0)

    second_a, second_b = Group(ra2), Group(rb2)
    for off in (2, -1, 1, 0):
        first_a[off].wait_recv()
        first_b[off].wait_recv()
        yc, xc = ring(y, off), ring(x, off)
        total_a = hp[yc, x, :, 0:512].astype(F32)
        total_b = hp[y, xc, :, 512:1024].astype(F32)
        for k in range(3):
            total_a += ra[k, yc].astype(F32)
            total_b += rb[k, xc].astype(F32)
        if off == 0:
            g_own[:, 0:512] = total_a
            g_own[:, 512:1024] = total_b
        else:
            k = OFFSETS.index(off)
            ha[k] = total_a.astype(BF16)
            hb[k] = total_b.astype(BF16)
            second_a.send(ha.at[k], ra2.at[k], dev("y", off))
            second_b.send(hb.at[k], rb2.at[k], dev("x", off))

    put = []
    for n, (keep, out) in enumerate(((gk_ref, gw_hbm), (uk_ref, uw_hbm))):
        pair[n].wait_recv()

        def sum_step(j, _, n=n, keep=keep):
            cols = pl.ds(pl.multiple_of(j * 128, 128), 128)
            for i in range(2):
                rows = slice(i * 128, (i + 1) * 128)
                total = w_send[n, rows, cols].astype(F32) + w_recv[n, rows, cols].astype(F32)
                w_out_v[n, rows, cols] = (total * keep[i, j].astype(F32)).astype(BF16)
            return 0

        lax.fori_loop(0, HID // 128, sum_step, 0)
        put.append(fetch(9 + n, w_out_v.at[n], out))

    second_a.wait_recv()
    second_b.wait_recv()
    for h in range(HEADS):
        cols = slice(h * HD, (h + 1) * HD)
        total = g_own[:, cols]
        buf = ra2 if h < 4 else rb2
        low = slice((h % 4) * HD, (h % 4 + 1) * HD)
        for k in range(3):
            total += buf[k, :, low].astype(F32)
        g_s[h * ROWS : (h + 1) * ROWS, :] = total.astype(BF16)

    val1, val2 = Group(vt_r), Group(vt2_r)
    key1, key2 = Group(kt_r), Group(kt2_r)
    delta = jnp.sum(out_t[...] * g_s[...].astype(F32).T, axis=0, keepdims=True)
    for off in (2, -1, 1, 0):
        yc = ring(y, off)
        rows = pl.ds(pl.multiple_of(yc * 320, 320), 320)
        prob_grad = nt(v_all[yc].reshape(320, HD), g_s[...])
        part = nn(p_low[rows, :], g_s[...]).astype(BF16)
        for i in range(4):
            vt_s[yc, i] = part[i * ROWS : (i + 1) * ROWS, :]
        if off != 0:
            val1.send(vt_s.at[yc], vt_r.at[OFFSETS.index(off)], dev("y", off))
        score = (p_f[rows, :] * (prob_grad - delta) * SCALE).astype(BF16)
        ds_s[rows, :] = score
        part = nn(score, q_s[...]).astype(BF16)
        for i in range(4):
            kt_s[yc, i] = part[i * ROWS : (i + 1) * ROWS, :]
        for k, o in enumerate(OFFSETS):
            xc = ring(x, o)
            key1.send(kt_s.at[yc, xc], kt_r.at[k, yc], dev("x", o))

    def q_step(t, _):
        cols = pl.ds(pl.multiple_of(t * 128, 128), 128)
        q_s[cols, :] = nn(k_t[...], ds_s[:, cols]).T.astype(BF16)
        return 0

    lax.fori_loop(0, QS // 128, q_step, 0)
    for h in range(HEADS):
        dq_ref[0, :, h * HD : (h + 1) * HD] = q_s[h * ROWS : (h + 1) * ROWS, :]

    def add_up(first, own, recv, buf, axis, keep_at, second, landing):
        first.wait_recv()
        for k, o in enumerate(OFFSETS):
            spot = ring(keep_at, o)
            total = own(spot).astype(F32)
            for j in range(3):
                total += recv[j, spot].astype(F32)
            buf[k] = total.astype(BF16)
            second.send(buf.at[k], landing.at[k], dev(axis, o))
        total = own(keep_at).astype(F32)
        for j in range(3):
            total += recv[j, keep_at].astype(F32)
        return total

    val_own = add_up(val1, lambda i: vt_s[y, i], vt_r, vt2_s, "x", x, val2, vt2_r)
    key_own = add_up(key1, lambda i: kt_s[i, x], kt_r, kt2_s, "y", y, key2, kt2_r)
    for own, second, landing, out in (
        (val_own, val2, vt2_r, dv_ref),
        (key_own, key2, kt2_r, dk_ref),
    ):
        second.wait_recv()
        for k in range(3):
            own += landing[k].astype(F32)
        out[0] = own.astype(BF16)

    for group in groups:
        group.wait_send()
    for copy in put:
        copy.wait()


def hand_on(*refs):
    sources, targets, through, (get_sem, put_sem) = refs[:5], refs[5:10], refs[10:15], refs[15:]
    parts = []
    for n in range(5):
        for i in range(PARTS if n < 2 else 1):
            rows = pl.ds(i * (FEAT // PARTS), FEAT // PARTS) if n < 2 else 0
            parts.append([ref.at[rows] for ref in (sources[n], through[n], targets[n])])
    gets = [
        pltpu.make_async_copy(part[0], part[1], get_sem.at[i]) for i, part in enumerate(parts)
    ]
    puts = [
        pltpu.make_async_copy(part[1], part[2], put_sem.at[i]) for i, part in enumerate(parts)
    ]
    for get in gets:
        get.start()
    for get, put in zip(gets, puts):
        get.wait()
        put.start()
    for put in puts:
        put.wait()


def on_device(
    ffn_input,
    gate_act,
    up_act,
    hidden_grad,
    stream_grad,
    w_gate,
    w_up,
    gate_keep,
    up_keep,
    w_out,
    queries,
    keys,
    values,
):
    hbm = pl.BlockSpec(memory_space=pl.ANY)
    vmem = pl.BlockSpec(memory_space=pltpu.VMEM)
    smem = pl.BlockSpec(memory_space=pltpu.SMEM)
    chunk_grid = (4, 4, ROWS)
    out_shape = (
        jax.ShapeDtypeStruct((FEAT, HID), BF16),
        jax.ShapeDtypeStruct((FEAT, HID), BF16),
        jax.ShapeDtypeStruct((1, ROWS, HEADS * HD), BF16),
        jax.ShapeDtypeStruct((1, ROWS, HD), BF16),
        jax.ShapeDtypeStruct((1, ROWS, HD), BF16),
    )
    results = pl.pallas_call(
        kernel,
        out_shape=out_shape,
        in_specs=[hbm, vmem, vmem, vmem, hbm, hbm, hbm, smem, smem, hbm, hbm, vmem, vmem],
        out_specs=(hbm, hbm, vmem, vmem, vmem),
        scratch_shapes=[
            pltpu.VMEM(chunk_grid + (HID,), BF16),
            pltpu.VMEM(chunk_grid + (HID,), BF16),
            pltpu.VMEM(chunk_grid + (HD,), BF16),
            pltpu.VMEM(chunk_grid + (HD,), BF16),
            pltpu.VMEM((2, FEAT, HID), BF16),
            pltpu.VMEM((SEQ, FEAT), BF16),
            pltpu.VMEM((FEAT, SEQ), BF16),
            pltpu.VMEM((HEADS * HD, FEAT), BF16),
            pltpu.VMEM((ROWS, HEADS * HD), BF16),
            pltpu.VMEM((QS, HD), BF16),
            pltpu.VMEM((4, ROWS, HD), BF16),
            pltpu.VMEM((4, 8, ROWS, HD), BF16),
            pltpu.VMEM((4, 7, ROWS, HD), BF16),
            pltpu.VMEM((4, 4, 2, ROWS, HD), BF16),
            pltpu.VMEM(chunk_grid + (HEADS * HD,), BF16),
            pltpu.VMEM((3, 4, ROWS, 512), BF16),
            pltpu.VMEM((3, 4, ROWS, 512), BF16),
            pltpu.VMEM((3, ROWS, 512), BF16),
            pltpu.VMEM((3, ROWS, 512), BF16),
            pltpu.VMEM((3, ROWS, 512), BF16),
            pltpu.VMEM((3, ROWS, 512), BF16),
            pltpu.VMEM((ROWS, HEADS * HD), F32),
            pltpu.VMEM((QS, HD), BF16),
            pltpu.VMEM((2, FEAT, HID), BF16),
            pltpu.VMEM((2, FEAT, HID), BF16),
            pltpu.VMEM((2, FEAT, HID), BF16),
            pltpu.VMEM((HD, SEQ), BF16),
            pltpu.VMEM((HD, SEQ), BF16),
            pltpu.VMEM((HD, QS), F32),
            pltpu.VMEM((SEQ, QS), F32),
            pltpu.VMEM((SEQ, QS), BF16),
            pltpu.VMEM((SEQ, QS), BF16),
            pltpu.VMEM(chunk_grid + (HD,), BF16),
            pltpu.VMEM(chunk_grid + (HD,), BF16),
            pltpu.VMEM((3, 4, ROWS, HD), BF16),
            pltpu.VMEM((3, 4, ROWS, HD), BF16),
            pltpu.VMEM((3, ROWS, HD), BF16),
            pltpu.VMEM((3, ROWS, HD), BF16),
            pltpu.VMEM((3, ROWS, HD), BF16),
            pltpu.VMEM((3, ROWS, HD), BF16),
            pltpu.SemaphoreType.DMA((N_GROUPS,)),
            pltpu.SemaphoreType.DMA((N_GROUPS,)),
            pltpu.SemaphoreType.DMA((11,)),
        ],
        compiler_params=pltpu.CompilerParams(
            collective_id=0, has_side_effects=True, vmem_limit_bytes=56 * 1024 * 1024
        ),
    )(
        ffn_input,
        gate_act,
        up_act,
        hidden_grad,
        stream_grad.reshape(16, ROWS, FEAT),
        w_gate,
        w_up,
        gate_keep,
        up_keep,
        w_out,
        queries,
        keys,
        values,
    )
    return pl.pallas_call(
        hand_on,
        out_shape=out_shape,
        in_specs=[hbm] * 5,
        out_specs=(hbm,) * 5,
        scratch_shapes=[pltpu.VMEM(shape.shape, BF16) for shape in out_shape]
        + [pltpu.SemaphoreType.DMA((2 * PARTS + 3,))] * 2,
        compiler_params=pltpu.CompilerParams(vmem_limit_bytes=60 * 1024 * 1024),
    )(*results)


def solution(mesh):
    placed = (
        P("dp", None, "row"),
        P("dp", "row", "col"),
        P("dp", "row", "col"),
        P("dp", "row", "col"),
        P("dp", None, "row"),
        P("row", "col"),
        P("row", "col"),
        P("row", "col"),
        P("row", "col"),
        P("col", "row"),
        P("dp", "row", "col"),
        P("dp", "row", "col"),
        P("dp", "row", "col"),
    )
    return jax.shard_map(
        on_device,
        mesh=mesh,
        in_specs=placed,
        out_specs=(
            P("row", "col"),
            P("row", "col"),
            P("dp", "row", "col"),
            P("dp", "row", "col"),
            P("dp", "row", "col"),
        ),
        check_vma=False,
    )
```

profile of v0, /device:TPU:2, one launch (start us, length us, event | category | flops | bytes accessed | tf_op | source)
XLA Modules:
  0.0 103.9 jit_solution(6464174293943677267)
XLA Ops:
  0.6 100.7 %shard_map.164 = (bf16[256,1792]{1,0:T(8,128)(2,1)}, bf16[256,1792]{1,0:T(8,128)(2,1)}, bf16[1,80,1024]{2,1,0:T(8,128)(2,1)}, bf16[1,80,128]{2,1,0:T(8,128)(2,1)}, bf16[1,80,128]{2,1,0:T(8,128)(2,1)}) custom-call(bf16[1,1280,256]{2,1,0:T(8,128)(2,1)} %ffn_hbm.1, bf16[1,80,1792]{2,1,0:T(8,128)(2,1)} %gate_ref.1, bf16[1,80,1792]{2,1,0:T(8,128)(2,1)} %up_ref.1, ...), custom_call_target="tpu_custom_call" | custom-call | tf_op jit(solution)/shard_map/pallas_call | solution.py:574
  101.4 2.5 %shard_map.165 = (bf16[256,1792]{1,0:T(8,128)(2,1)}, bf16[256,1792]{1,0:T(8,128)(2,1)}, bf16[1,80,1024]{2,1,0:T(8,128)(2,1)}, bf16[1,80,128]{2,1,0:T(8,128)(2,1)}, bf16[1,80,128]{2,1,0:T(8,128)(2,1)}) custom-call(bf16[256,1792]{1,0:T(8,128)(2,1)} %get-tuple-element.10.refs_0_, bf16[256,1792]{1,0:T(8,128)(2,1)} %get-tuple-element.11.refs_1_, ...), custom_call_target="tpu_custom_call" | custom-call | tf_op jit(solution)/shard_map/pallas_call | solution.py:642
where the time goes:
time: 104 us
  Pallas kernels  103 us (99%)
    pallas_call x1, Pallas kernels, on_device(): pl.pallas_call(kernel, out_shape=out_shape, in_specs=[hbm, vmem, vmem, vm...  101 us
    pallas_call x1, Pallas kernels, on_device(): pl.pallas_call(hand_on, out_shape=out_shape, in_specs=[hbm] * 5, out_spec...  2.52 us

commit v1 on v0

--- a/solution.py
+++ b/solution.py
@@ -26,8 +26,8 @@
 OFFSETS = (-1, 1, 2)
 
 QUARTERS = (
-    ((0, 0), (0, -1), (-1, 0), (-1, -1)),
-    ((0, 1), (1, 0), (-1, 1), (1, -1)),
+    ((0, 0), (0, -1), (-1, 0), (0, 1)),
+    ((1, 0), (-1, -1), (-1, 1), (1, -1)),
     ((0, 2), (2, 0), (1, 2), (2, 1)),
     ((1, 1), (-1, 2), (2, -1), (2, 2)),
 )
@@ -344,7 +344,7 @@
             across[n, first].wait_recv()
             block = at(n, first, -d)
             far[n, part].send(block, block, dev(arrays[n][2], d))
-        if first == -1:
+        if first == 0:
             input_terms(0)
         if first == 1:
             input_terms(1)

time: 104 us -> 104 us (level)
  no operation moved by 1% of the time
where the time goes in v1:
time: 104 us
  Pallas kernels  103 us (99%)
    pallas_call x1, Pallas kernels, on_device(): pl.pallas_call(kernel, out_shape=out_shape, in_specs=[hbm, vmem, vmem, vm...  101 us
    pallas_call x1, Pallas kernels, on_device(): pl.pallas_call(hand_on, out_shape=out_shape, in_specs=[hbm] * 5, out_spec...  2.52 us

profile of v1, /device:TPU:2, one launch (start us, length us, event | category | flops | bytes accessed | tf_op | source)
XLA Modules:
  0.0 103.7 jit_solution(15999880916677308251)
XLA Ops:
  0.6 100.6 %shard_map.164 = (bf16[256,1792]{1,0:T(8,128)(2,1)}, bf16[256,1792]{1,0:T(8,128)(2,1)}, bf16[1,80,1024]{2,1,0:T(8,128)(2,1)}, bf16[1,80,128]{2,1,0:T(8,128)(2,1)}, bf16[1,80,128]{2,1,0:T(8,128)(2,1)}) custom-call(bf16[1,1280,256]{2,1,0:T(8,128)(2,1)} %ffn_hbm.1, bf16[1,80,1792]{2,1,0:T(8,128)(2,1)} %gate_ref.1, bf16[1,80,1792]{2,1,0:T(8,128)(2,1)} %up_ref.1, ...), custom_call_target="tpu_custom_call" | custom-call | tf_op jit(solution)/shard_map/pallas_call | solution.py:574
  101.2 2.5 %shard_map.165 = (bf16[256,1792]{1,0:T(8,128)(2,1)}, bf16[256,1792]{1,0:T(8,128)(2,1)}, bf16[1,80,1024]{2,1,0:T(8,128)(2,1)}, bf16[1,80,128]{2,1,0:T(8,128)(2,1)}, bf16[1,80,128]{2,1,0:T(8,128)(2,1)}) custom-call(bf16[256,1792]{1,0:T(8,128)(2,1)} %get-tuple-element.10.refs_0_, bf16[256,1792]{1,0:T(8,128)(2,1)} %get-tuple-element.11.refs_1_, ...), custom_call_target="tpu_custom_call" | custom-call | tf_op jit(solution)/shard_map/pallas_call | solution.py:642
